TPU v7x, 512 devices: a whole 4x4x16 slice. The times are simulated.
512 devices in a mesh: tile: 32 (over z, core), tp: 16 (over y, x).
Axes of the slice: x: 4, y: 4, z: 16, core: 2. Of those that a mesh axis runs over, the one named last changes fastest.
Arguments:
- tokens: bfloat16 [16384, 1280], P('tile', 'tp'), may hold values from -6 to 6
- mask: int32 [32, 512], P('tile'), may hold values from 0 to 1, as said below
- ln1_gain: float32 [1280], replicated, may hold values from 0.1 to 1.9
- w_query: bfloat16 [1280, 1280], P(None, 'tp'), may hold values from -0.15625 to 0.15625
- w_key: bfloat16 [1280, 1280], P(None, 'tp'), may hold values from -0.15625 to 0.15625
- w_value: bfloat16 [1280, 1280], P(None, 'tp'), may hold values from -0.15625 to 0.15625
- w_out: bfloat16 [1280, 1280], P('tp'), may hold values from -0.15625 to 0.15625
- ln2_gain: float32 [1280], replicated, may hold values from 0.1 to 1.9
- w_in: bfloat16 [1280, 5120], P(None, 'tp'), may hold values from -0.15625 to 0.15625
- w_back: bfloat16 [5120, 1280], P('tp'), may hold values from -0.078125 to 0.078125
Outputs:
- encoded: bfloat16 [16384, 1280], P('tile', 'tp')
Inputs may be any that keep to these rules, and one draw needn't show every extreme that they name: `mask`: tile t has between 128 and 384 visible tokens, tile 0 exactly 384, and the visible counts of tiles t and t + 16 add up to 512.
All inputs are finite; a program needn't handle non-finite values.
Results may differ from a plain program's by a relative error of at most 0.009.
Values may be sent and summed in bfloat16 or wider, within the bound.
A program may use at most 64 MiB of HBM per device.

v0:
```python
import jax
import jax.numpy as jnp
from jax import lax
from jax.sharding import PartitionSpec as P

HEAD_DIM = 80


def with_halo(block, sides, width):
    for axis, dim in sides:
        count = lax.axis_size(axis)
        forward = [(i, i + 1) for i in range(count - 1)]
        backward = [(target, source) for source, target in forward]
        low = lax.ppermute(
            lax.slice_in_dim(block, block.shape[dim] - width, None, axis=dim), axis, forward
        )
        high = lax.ppermute(lax.slice_in_dim(block, 0, width, axis=dim), axis, backward)
        block = jnp.concatenate([low, block, high], axis=dim)
    return block


def normalize(rows, gain):
    rows = rows.astype(jnp.float32)
    mean = jnp.mean(rows, axis=-1, keepdims=True)
    centred = rows - mean
    var = jnp.mean(centred * centred, axis=-1, keepdims=True)
    return centred * lax.rsqrt(var + 1e-06) * gain


def body(tokens, mask, ln1_gain, w_query, w_key, w_value, w_out, ln2_gain, w_in, w_back):
    tile_rows = tokens.shape[0]
    most = 3 * tile_rows // 4
    visible_here = mask[0]
    count = jnp.sum(visible_here)
    order = jnp.argsort(1 - visible_here, stable=True)[:most]
    slots = jnp.arange(most, dtype=jnp.int32)
    valid = slots < count
    rows = tokens[order]
    whole = lax.all_gather(rows, "tp", axis=1, tiled=True)
    a_one = normalize(whole, ln1_gain).astype(jnp.bfloat16)
    query = jnp.dot(a_one, w_query, preferred_element_type=jnp.float32).astype(jnp.bfloat16)
    keys = jnp.dot(a_one, w_key, preferred_element_type=jnp.float32).astype(jnp.bfloat16)
    values = jnp.dot(a_one, w_value, preferred_element_type=jnp.float32).astype(jnp.bfloat16)
    heads_here = query.shape[1] // HEAD_DIM
    stacked = jnp.stack([keys, values])
    flags = valid.astype(jnp.int32).reshape(1, most)
    near, near_flags = (
        with_halo(stacked, (("tile", 1),), most),
        with_halo(flags, (("tile", 1),), most),
    )
    near_keys = near[0].reshape(3 * most, heads_here, HEAD_DIM)
    near_values = near[1].reshape(3 * most, heads_here, HEAD_DIM)
    key_live = near_flags[0][None, None, :] > 0

    def attend(block_query):
        scores = jnp.einsum(
            "qhd,khd->hqk", block_query, near_keys, preferred_element_type=jnp.float32
        )
        scores = scores / jnp.sqrt(jnp.float32(HEAD_DIM))
        scores = jnp.where(key_live, scores, jnp.float32(-1e30))
        probs = jax.nn.softmax(scores, axis=-1).astype(jnp.bfloat16)
        result = jnp.einsum("hqk,khd->qhd", probs, near_values, preferred_element_type=jnp.float32)
        return result.astype(jnp.bfloat16)

    blocked = query.reshape(most // most, most, heads_here, HEAD_DIM)
    mixed = lax.map(attend, blocked).reshape(most, heads_here * HEAD_DIM)
    partial_out = jnp.dot(mixed, w_out, preferred_element_type=jnp.float32)
    attn = lax.psum_scatter(partial_out, "tp", scatter_dimension=1, tiled=True)
    hidden = (rows.astype(jnp.float32) + attn).astype(jnp.bfloat16)
    full_hidden = lax.all_gather(hidden, "tp", axis=1, tiled=True)
    a_two = normalize(full_hidden, ln2_gain).astype(jnp.bfloat16)
    inner = jax.nn.gelu(jnp.dot(a_two, w_in, preferred_element_type=jnp.float32)).astype(
        jnp.bfloat16
    )
    back = jnp.dot(inner, w_back, preferred_element_type=jnp.float32)
    summed = lax.psum_scatter(back, "tp", scatter_dimension=1, tiled=True)
    finished = (hidden.astype(jnp.float32) + summed).astype(jnp.bfloat16)
    kept = jnp.where(valid[:, None], finished, jnp.zeros_like(finished))
    output = jnp.zeros_like(tokens)
    return output.at[order].set(kept)


def solution(mesh):
    placed = (
        P("tile", "tp"),
        P("tile", None),
        P(),
        P(None, "tp"),
        P(None, "tp"),
        P(None, "tp"),
        P("tp", None),
        P(),
        P(None, "tp"),
        P("tp", None),
    )
    return jax.shard_map(
        body, mesh=mesh, in_specs=placed, out_specs=P("tile", "tp"), check_vma=False
    )
```

profile of v0, /device:TPU:2, one launch (start us, length us, event | category | flops | bytes accessed | tf_op | source)
XLA Modules:
  0.0 283.3 jit_solution(16501979167056648653)
XLA Ops:
  6.5 1.5 fusion.61
  8.0 3.8 %sort.17 = (s32[512]{0:T(512)}, s32[512]{0:T(512)S(1)}) sort(s32[512]{0:T(512)S(1)} %bitcast.30, s32[512]{0:T(512)S(1)} %iota.12), dimensions={0}, to_apply=%region_0.0 | sort | flops 4608 | bytes 8192 | tf_op jit(solution)/shard_map/jit(argsort)/sort | solution.py:35
  11.8 1.0 copy.22
  12.8 1.4 gather_fusion
  14.3 0.1 copy.23
  14.4 27.6 %all-gather = bf16[384,1280]{0,1:T(8,128)(2,1)S(1)} all-gather(bf16[384,80]{0,1:T(8,128)(2,1)S(1)} %copy.23), channel_id=2, replica_groups=mesh['tile'=32,'tp'=16] {'tp'}, dimensions={1}, use_global_device_ids=true | all-gather | bytes 1044480 | tf_op jit(solution)/shard_map/all_gather | solution.py:39
  42.0 0.2 convert_reduce_fusion.1
  42.2 0.3 fusion.7
  42.6 0.5 fusion.14
  43.1 0.5 fusion.13
  43.6 1.3 collective-permute-start.1
  44.9 3.0 %collective-permute-start = (bf16[2,384,80]{1,2,0:T(8,128)(2,1)S(1)}, bf16[2,384,80]{1,2,0:T(8,128)(2,1)S(1)}, u32[]{:S(2)}, u32[]{:S(2)}) collective-permute-start(bf16[2,384,80]{1,2,0:T(8,128)(2,1)S(1)} %pad_maximum_fusion.1), channel_id=1, source_target_pairs={{0,16},{16,32},{32,48},{48,64},{64,80},{80,96},{96,112},{112,128},... | collective-permute-start | bytes 368648 | tf_op jit(solution)/shard_map/ppermute | solution.py:14
  47.9 0.6 compare_convert_fusion
  48.6 1.3 collective-permute-start.3
  49.9 3.0 %collective-permute-start.2 = (s32[1,384]{1,0:T(1,128)S(1)}, s32[1,384]{1,0:T(1,128)S(1)}, u32[]{:S(2)}, u32[]{:S(2)}) collective-permute-start(s32[1,384]{1,0:T(1,128)S(1)} %compare_convert_fusion), channel_id=1, source_target_pairs={{0,16},{16,32},{32,48},{48,64},{64,80},{80,96},{96,112},{112,128},... | collective-permute-start | bytes 4616 | tf_op jit(solution)/shard_map/ppermute | solution.py:14
  52.9 0.8 collective-permute-done.2
  53.8 2.1 select_reduce_fusion
  55.9 1.9 fusion.10
  57.9 3.8 %fusion.12 = f32[384,1280]{0,1:T(8,128)} fusion(bf16[80,1280]{1,0:T(8,128)(2,1)S(1)} %copy-done.5, f32[384,1152]{1,0:T(8,128)} %get-tuple-element.28, f32[384]{0:T(512)S(1)} %fusion.10, f32[384]{0:T(512)S(1)} %get-tuple-element.26, pred[1152]{0:T(1024)(128)(4,1)S(1)} %compare_reduce_fusion, bf16[2,1152,80]{1,2,0:T(8,128)(2,1)S(1)} %pad_maximum_fusion), kind=kOutput, calls=%fused_computation.26 | convolution fusion | flops 151222272 | bytes 4130816 | tf_op jit(solution)/shard_map/dot_general | solution.py:67
  61.7 0.0 reduce-scatter.9.cloned.1.call-start
  61.7 94.3 %reduce-scatter.7.cloned.1.call-done = f32[384,80]{0,1:T(8,128)} async-done(((f32[384,1280]{0,1:T(8,128)}), f32[384,80]{0,1:T(8,128)}) %reduce-scatter.7.cloned.1.call-update) | async-done | bytes 122896
  156.0 1.0 copy.24
  157.1 0.1 copy.25
  157.2 23.1 %all_gather.7 = bf16[384,1280]{0,1:T(8,128)(2,1)S(1)} all-gather(bf16[384,80]{0,1:T(8,128)(2,1)S(1)} %copy.25), channel_id=1, replica_groups=mesh['tile'=32,'tp'=16] {'tp'}, dimensions={1}, use_global_device_ids=true | all-gather | bytes 1044480 | tf_op jit(solution)/shard_map/all_gather | solution.py:70
  180.3 0.2 convert_reduce_fusion
  180.5 0.3 fusion.4
  180.9 2.7 fusion.39
  183.6 0.6 iota_compare_fusion
  184.3 88.9 %reduce-scatter.9.cloned.1.call-done = f32[384,80]{0,1:T(8,128)} async-done(((f32[384,1280]{0,1:T(8,128)}), f32[384,80]{0,1:T(8,128)}) %reduce-scatter.9.cloned.1.call-update) | async-done | bytes 122896
  273.1 1.0 copy.26
  274.1 1.6 scatter_custom_fusion
  275.8 0.7 copy.27
  (33 shorter events, 0.2 us)
Async XLA Ops:
  6.5 174.3 %copy-start = (bf16[320,1280]{1,0:T(8,128)(2,1)S(1)}, bf16[320,1280]{1,0:T(8,128)(2,1)}, u32[]{:S(2)}) copy-start(bf16[320,1280]{1,0:T(8,128)(2,1)} %param.19) | copy-start | bytes 2457604
  6.5 149.5 %reduce-scatter.7.cloned.1.call-start = ((), (), s32[]{:S(2)}) async-start(), calls=%async_computation.2 | async-start | bytes 2088960
  12.8 29.8 %copy-start.2 = (bf16[1280,80]{0,1:T(8,128)(2,1)S(1)}, bf16[1280,80]{0,1:T(8,128)(2,1)}, u32[]{:S(2)}) copy-start(bf16[1280,80]{0,1:T(8,128)(2,1)} %param.15) | copy-start | bytes 614404
  12.8 29.8 %copy-start.6 = (f32[1280]{0:T(1024)S(1)}, f32[1280]{0:T(1024)}, u32[]{:S(2)}) copy-start(f32[1280]{0:T(1024)} %param.12) | copy-start | bytes 15364
  42.0 1.1 copy-start.3
  43.1 10.7 %copy-start.4 = (bf16[1280,80]{0,1:T(8,128)(2,1)S(1)}, bf16[1280,80]{0,1:T(8,128)(2,1)}, u32[]{:S(2)}) copy-start(bf16[1280,80]{0,1:T(8,128)(2,1)} %param.13) | copy-start | bytes 614404
  43.6 10.2 %collective-permute-start.1 = (bf16[2,384,80]{1,2,0:T(8,128)(2,1)S(1)}, bf16[2,384,80]{1,2,0:T(8,128)(2,1)S(1)}, u32[]{:S(2)}, u32[]{:S(2)}) collective-permute-start(bf16[2,384,80]{1,2,0:T(8,128)(2,1)S(1)} %pad_maximum_fusion.1), channel_id=1, source_target_pairs={{16,0},{32,16},{48,32},{64,48},{80,64},{96,80},{112,96},{128,112},... | collective-permute-start | bytes 368648 | tf_op jit(solution)/shard_map/ppermute | solution.py:17
  44.9 8.9 %collective-permute-start = (bf16[2,384,80]{1,2,0:T(8,128)(2,1)S(1)}, bf16[2,384,80]{1,2,0:T(8,128)(2,1)S(1)}, u32[]{:S(2)}, u32[]{:S(2)}) collective-permute-start(bf16[2,384,80]{1,2,0:T(8,128)(2,1)S(1)} %pad_maximum_fusion.1), channel_id=1, source_target_pairs={{0,16},{16,32},{32,48},{48,64},{64,80},{80,96},{96,112},{112,128},... | collective-permute-start | bytes 368648 | tf_op jit(solution)/shard_map/ppermute | solution.py:14
  48.6 4.3 %collective-permute-start.3 = (s32[1,384]{1,0:T(1,128)S(1)}, s32[1,384]{1,0:T(1,128)S(1)}, u32[]{:S(2)}, u32[]{:S(2)}) collective-permute-start(s32[1,384]{1,0:T(1,128)S(1)} %compare_convert_fusion), channel_id=1, source_target_pairs={{16,0},{32,16},{48,32},{64,48},{80,64},{96,80},{112,96},{128,112},... | collective-permute-start | bytes 4616 | tf_op jit(solution)/shard_map/ppermute | solution.py:17
  49.9 3.8 %collective-permute-start.2 = (s32[1,384]{1,0:T(1,128)S(1)}, s32[1,384]{1,0:T(1,128)S(1)}, u32[]{:S(2)}, u32[]{:S(2)}) collective-permute-start(s32[1,384]{1,0:T(1,128)S(1)} %compare_convert_fusion), channel_id=1, source_target_pairs={{0,16},{16,32},{32,48},{48,64},{64,80},{80,96},{96,112},{112,128},... | collective-permute-start | bytes 4616 | tf_op jit(solution)/shard_map/ppermute | solution.py:14
  53.8 4.0 %copy-start.5 = (bf16[80,1280]{1,0:T(8,128)(2,1)S(1)}, bf16[80,1280]{1,0:T(8,128)(2,1)}, u32[]{:S(2)}) copy-start(bf16[80,1280]{1,0:T(8,128)(2,1)} %param.16) | copy-start | bytes 614404
  61.7 119.2 %copy-start.1 = (bf16[1280,320]{0,1:T(8,128)(2,1)S(1)}, bf16[1280,320]{0,1:T(8,128)(2,1)}, u32[]{:S(2)}) copy-start(bf16[1280,320]{0,1:T(8,128)(2,1)} %param.18) | copy-start | bytes 2457604
  61.7 119.2 %copy-start.7 = (f32[1280]{0:T(1024)S(1)}, f32[1280]{0:T(1024)}, u32[]{:S(2)}) copy-start(f32[1280]{0:T(1024)} %param.17) | copy-start | bytes 15364
  61.7 211.4 %reduce-scatter.9.cloned.1.call-start = ((), (), s32[]{:S(2)}) async-start(), calls=%async_computation.3 | async-start | bytes 2088960
Sparse Core Ops, SparseCore 0:
  61.8 94.1 reduce-scatter.6
  183.7 89.3 reduce-scatter.8
where the time goes:
time: 284 us; the launch traced here: 283 us
  waiting for transfers between devices  184 us (65%)
  blocking collectives  50.7 us (18%)
  between operations  13.6 us (5%)
  other arithmetic  11.2 us (4%)
  matrix products  9.58 us (3%)
  starting transfers between devices  8.7 us (3%)
  local copies, waits for them, and re-layouts  5.5 us (2%)
    unnamed x4, waiting for transfers between devices  183 us
    all_gather x1, blocking collectives, body(): whole = lax.all_gather(rows, 'tp', axis=1, tiled=True)  27.6 us
    all_gather x1, blocking collectives, body(): full_hidden = lax.all_gather(hidden, 'tp', axis=1, tiled=True)  23.1 us
    ppermute x2, starting transfers between devices, with_halo(): lax.ppermute(lax.slice_in_dim(block, block.shape[dim] - width, None, axis...  6.07 us
  transfers between devices with their start and end apart: 6, of which 3 were waited for; matrix products, arithmetic and copies ran while one was open for 0% of the time, Pallas kernels for 0%

commit v1 on v0

v1 whole, which is shorter than its diff:
```python
import functools

import jax
import jax.numpy as jnp
from jax import lax
from jax.experimental import pallas as pl
from jax.experimental.pallas import tpu as pltpu
from jax.sharding import PartitionSpec as P

MESH = pl.DeviceIdType.MESH
D = 1280
FB = 320
HD = 80
SIDE = 4
ROWS = 512
LIVE = 384
CUT = 48
KB = 96
KV = 176
EPS = 1e-06
LOW = -1e30
EXPF = 1.4426950408889634 / (80.0**0.5)
BF = jnp.bfloat16
F32 = jnp.float32


def dot(a, b, dims=((1,), (0,))):
    return lax.dot_general(a, b, (dims, ((), ())), preferred_element_type=F32)


def kernel(
    tok, mask, gain1, gain2, wq, wk, wv, wo, wi, wb, out,
    x1, x2, norm, part, ra, rb, ta, tb, ua, ub, kv, qa, score, prob, place,
    wqkv_t, wo_t, wi_t, wb_t, g1, g2, send, recv,
):
    tp = lax.axis_index("tp")
    tile = lax.axis_index("tile")
    tiles = lax.axis_size("tile")
    xx, yy = lax.rem(tp, SIDE), lax.div(tp, SIDE)

    def xpeer(d):
        return {"tp": yy * SIDE + lax.rem(xx + d, SIDE)}

    def ypeer(d):
        return {"tp": lax.rem(yy + d, SIDE) * SIDE + xx}

    after = {"tile": lax.rem(tile + 1, tiles)}
    before = {"tile": lax.rem(tile + tiles - 1, tiles)}
    peers = [xpeer(d) for d in (1, 2, 3)] + [ypeer(d) for d in (1, 2, 3)] + [after, before]

    barrier = pltpu.get_barrier_semaphore()
    for peer in peers:
        pl.semaphore_signal(barrier, inc=1, device_id=peer, device_id_type=MESH)

    count_sems = [0]

    def push(src, dst, peer):
        k = count_sems[0]
        count_sems[0] += 1
        copy = pltpu.make_async_remote_copy(
            src_ref=src, dst_ref=dst, send_sem=send.at[k], recv_sem=recv.at[k],
            device_id=peer, device_id_type=MESH,
        )
        copy.start()
        return copy

    def finish(copies):
        for copy in copies:
            copy.wait()

    low, high = pl.ds(0, CUT), pl.ds(CUT, HD - CUT)

    flags = mask[...].astype(F32).astype(BF)
    row_i = lax.broadcasted_iota(jnp.int32, (ROWS, ROWS), 0)
    col_i = lax.broadcasted_iota(jnp.int32, (ROWS, ROWS), 1)
    upper = (row_i <= col_i).astype(F32).astype(BF)
    running = dot(jnp.broadcast_to(flags, (16, ROWS)), upper)[0:1, :]
    total = running[0:1, ROWS - 1 : ROWS]
    slot = jnp.where(mask[...] > 0, running - 1.0, -1.0).astype(jnp.int32)
    at = lax.broadcasted_iota(jnp.int32, (LIVE, ROWS), 0) == slot
    place[...] = at.astype(F32).astype(BF)
    tok_t = tok[...].astype(F32).T.astype(BF)
    mine = dot(tok_t, place[...], ((1,), (1,))).astype(BF)
    x1[yy, xx] = mine

    pl.semaphore_wait(barrier, len(peers))

    def gather(buf):
        first = [push(buf.at[yy, xx, low], buf.at[yy, xx, low], xpeer(d)) for d in (1, 2, 3)]
        first += [push(buf.at[yy, xx, high], buf.at[yy, xx, high], ypeer(d)) for d in (1, 2, 3)]
        return first

    def gather_rest(buf, first):
        finish(first)
        rest = [push(buf.at[yy, :, low], buf.at[yy, :, low], ypeer(d)) for d in (1, 2, 3)]
        rest += [push(buf.at[:, xx, high], buf.at[:, xx, high], xpeer(d)) for d in (1, 2, 3)]
        return rest

    first = gather(x1)

    for i, w in enumerate((wq, wk, wv)):
        wqkv_t[HD * i : HD * (i + 1), :] = w[...].astype(F32).T.astype(BF)
    for i in range(D // 128):
        cols = slice(128 * i, 128 * (i + 1))
        g1[cols, :] = jnp.broadcast_to(gain1[:, cols], (128, 128)).T
        g2[cols, :] = jnp.broadcast_to(gain2[:, cols], (128, 128)).T
    rest = gather_rest(x1, first)
    wo_t[...] = wo[...].astype(F32).T.astype(BF)
    for i in range(4):
        wi_t[:, FB * i : FB * (i + 1)] = wi[FB * i : FB * (i + 1), :].astype(F32).T.astype(BF)
        wb_t[FB * i : FB * (i + 1), :] = wb[:, FB * i : FB * (i + 1)].astype(F32).T.astype(BF)
    finish(rest)

    def normalize(buf, gain):
        def shard(i):
            return buf[i // SIDE, i % SIDE].astype(F32)

        total = jnp.zeros((HD, LIVE), F32)
        for i in range(16):
            total += shard(i)
        mean = jnp.sum(total, axis=0, keepdims=True) * (1.0 / D)
        square = jnp.zeros((HD, LIVE), F32)
        for i in range(16):
            centred = shard(i) - mean
            square += centred * centred
        var = jnp.sum(square, axis=0, keepdims=True) * (1.0 / D)
        scale = lax.rsqrt(var + EPS)
        for i in range(16):
            g = gain[HD * i : HD * (i + 1), :]
            g = jnp.concatenate([g, g, g], axis=1)
            norm[HD * i : HD * (i + 1), :] = ((shard(i) - mean) * scale * g).astype(BF)

    normalize(x1, g1)
    qkv = dot(wqkv_t[...], norm[...]).astype(BF)
    valid = lax.broadcasted_iota(jnp.int32, (16, LIVE), 1).astype(F32) < total
    top = lax.broadcasted_iota(jnp.int32, (16, LIVE), 0) == 0
    qa[0:HD, :] = qkv[0:HD]
    qa[HD:KB, :] = top.astype(F32).astype(BF)
    kv[1, 0:HD, :] = qkv[HD : 2 * HD]
    kv[1, HD:KB, :] = jnp.where(valid, 0.0, jnp.where(top, LOW, 0.0)).astype(BF)
    kv[1, KB:KV, :] = qkv[2 * HD :]
    halo = [push(kv.at[1], kv.at[0], after), push(kv.at[1], kv.at[2], before)]
    finish(halo)
    edge = jnp.where(top, LOW, 0.0)
    for i, at_edge in ((0, tile == 0), (2, tile == tiles - 1)):
        off = jnp.where(at_edge, 1.0, 0.0).astype(F32)
        kv[i, HD:KB, :] = (kv[i, HD:KB, :].astype(F32) + edge * off).astype(BF)

    best = jnp.full((8, LIVE), LOW, F32)
    for i in range(3):
        keys = kv[i, 0:KB, :].astype(F32).T.astype(BF)
        s = dot(keys, qa[...])
        score[i] = s
        best = jnp.maximum(best, jnp.max(s.reshape(LIVE // 8, 8, LIVE), axis=0))
    best = jnp.max(best, axis=0, keepdims=True)
    weight = jnp.zeros((8, LIVE), F32)
    mixed = jnp.zeros((HD, LIVE), F32)
    for i in range(3):
        p = jnp.exp2((score[i] - best) * EXPF)
        weight += jnp.sum(p.reshape(LIVE // 8, 8, LIVE), axis=0)
        prob[i] = p.astype(BF)
        mixed += dot(kv[i, KB:KV, :], prob[i])
    weight = jnp.sum(weight, axis=0, keepdims=True)
    o = (mixed / weight).astype(BF)

    def scatter(n):
        first = [push(part.at[n, lax.rem(yy + d, SIDE), :, low], ra.at[n, d - 1], ypeer(d)) for d in (1, 2, 3)]
        first += [push(part.at[n, :, lax.rem(xx + d, SIDE), high], rb.at[n, d - 1], xpeer(d)) for d in (1, 2, 3)]
        finish(first)
        sum_a = part[n, yy, :, low].astype(F32)
        sum_b = part[n, :, xx, high].astype(F32)
        for d in range(3):
            sum_a += ra[n, d].astype(F32)
            sum_b += rb[n, d].astype(F32)
        ta[n] = sum_a.astype(BF)
        tb[n] = sum_b.astype(BF)
        rest = [push(ta.at[n, lax.rem(xx + d, SIDE)], ua.at[n, d - 1], xpeer(d)) for d in (1, 2, 3)]
        rest += [push(tb.at[n, lax.rem(yy + d, SIDE)], ub.at[n, d - 1], ypeer(d)) for d in (1, 2, 3)]
        finish(rest)
        sum_a = ta[n, xx].astype(F32)
        sum_b = tb[n, yy].astype(F32)
        for d in range(3):
            sum_a += ua[n, d].astype(F32)
            sum_b += ub[n, d].astype(F32)
        return jnp.concatenate([sum_a, sum_b], axis=0)

    for i in range(SIDE):
        block = dot(wo_t[FB * i : FB * (i + 1), :], o).astype(BF)
        for j in range(SIDE):
            part[0, i, j] = block[HD * j : HD * (j + 1)]
    hidden = (x1[yy, xx].astype(F32) + scatter(0)).astype(BF)
    x2[yy, xx] = hidden
    finish(gather_rest(x2, gather(x2)))
    normalize(x2, g2)
    inner = jax.nn.gelu(dot(wi_t[...], norm[...])).astype(BF)
    for i in range(SIDE):
        block = dot(wb_t[FB * i : FB * (i + 1), :], inner).astype(BF)
        for j in range(SIDE):
            part[1, i, j] = block[HD * j : HD * (j + 1)]
    done = (x2[yy, xx].astype(F32) + scatter(1)).astype(BF)
    out[...] = dot(done, place[...]).T.astype(BF)


def body(tokens, mask, ln1_gain, w_query, w_key, w_value, w_out, ln2_gain, w_in, w_back):
    v = pl.BlockSpec(memory_space=pltpu.VMEM)
    n_sem = 64
    return pl.pallas_call(
        kernel,
        out_shape=jax.ShapeDtypeStruct(tokens.shape, tokens.dtype),
        in_specs=[v] * 10,
        out_specs=v,
        scratch_shapes=[
            pltpu.VMEM((SIDE, SIDE, HD, LIVE), BF),
            pltpu.VMEM((SIDE, SIDE, HD, LIVE), BF),
            pltpu.VMEM((D, LIVE), BF),
            pltpu.VMEM((2, SIDE, SIDE, HD, LIVE), BF),
            pltpu.VMEM((2, 3, SIDE, CUT, LIVE), BF),
            pltpu.VMEM((2, 3, SIDE, HD - CUT, LIVE), BF),
            pltpu.VMEM((2, SIDE, CUT, LIVE), BF),
            pltpu.VMEM((2, SIDE, HD - CUT, LIVE), BF),
            pltpu.VMEM((2, 3, CUT, LIVE), BF),
            pltpu.VMEM((2, 3, HD - CUT, LIVE), BF),
            pltpu.VMEM((3, KV, LIVE), BF),
            pltpu.VMEM((KB, LIVE), BF),
            pltpu.VMEM((3, LIVE, LIVE), F32),
            pltpu.VMEM((3, LIVE, LIVE), BF),
            pltpu.VMEM((LIVE, ROWS), BF),
            pltpu.VMEM((3 * HD, D), BF),
            pltpu.VMEM((D, HD), BF),
            pltpu.VMEM((FB, D), BF),
            pltpu.VMEM((D, FB), BF),
            pltpu.VMEM((D, 128), F32),
            pltpu.VMEM((D, 128), F32),
            pltpu.SemaphoreType.DMA((n_sem,)),
            pltpu.SemaphoreType.DMA((n_sem,)),
        ],
        compiler_params=pltpu.CompilerParams(
            collective_id=0, has_side_effects=True, vmem_limit_bytes=52 * 2**20
        ),
    )(tokens, mask, ln1_gain.reshape(1, D), ln2_gain.reshape(1, D), w_query, w_key, w_value, w_out, w_in, w_back)


def solution(mesh):
    placed = (
        P("tile", "tp"),
        P("tile", None),
        P(),
        P(None, "tp"),
        P(None, "tp"),
        P(None, "tp"),
        P("tp", None),
        P(),
        P(None, "tp"),
        P("tp", None),
    )
    return jax.shard_map(
        body, mesh=mesh, in_specs=placed, out_specs=P("tile", "tp"), check_vma=False
    )
```

time: 284 us -> 74.3 us (0.26)
  waiting for transfers between devices: 184 us -> 0 us
  Pallas kernels: 0 us -> 69 us
  blocking collectives: 50.7 us -> 0 us
  between operations: 13.6 us -> 0.08 us
  other arithmetic: 11.2 us -> 0 us
  matrix products: 9.58 us -> 0 us
  starting transfers between devices: 8.7 us -> 0 us
    unnamed x4 -> x0, waiting for transfers between devices: 183 us -> none
    pallas_call x0 -> x1, Pallas kernels: none -> 69 us  [body(): pl.pallas_call(kernel, out_shape=jax.ShapeDtypeStruct(tokens.shape, token...]
    all_gather x2 -> x0, blocking collectives: 50.7 us -> none  [the longest x1 27.6 us: body(): whole = lax.all_gather(rows, 'tp', axis=1, tiled=True)]
    dot_general x5 -> x0, matrix products: 9.58 us -> none  [the longest x1 3.79 us: body(): partial_out = jnp.dot(mixed, w_out, preferred_element_type=jnp.float32)]
    ppermute x4 -> x0, starting transfers between devices: 8.65 us -> none  [the longest x2 6.07 us: with_halo(): lax.ppermute(lax.slice_in_dim(block, block.shape[dim] - width, None, axis...]
    reduce_sum x6 -> x0, other arithmetic: 4.46 us -> none  [the longest x1 1.91 us: attend(): probs = jax.nn.softmax(scores, axis=-1).astype(jnp.bfloat16)]
    sort x1 -> x0, other arithmetic: 3.77 us -> none  [body(): order = jnp.argsort(1 - visible_here, stable=True)[:most]]
  transfers between devices with their start and end apart: 6 -> 0, of which waited for: 3 -> 0; matrix products, arithmetic and copies ran while one was open for 0% -> 0% of each run, Pallas kernels for 0% -> 0%
where the time goes in v1:
time: 74.3 us; the launch traced here: 74 us
  Pallas kernels  69 us (93%)
  local copies, waits for them, and re-layouts  4.97 us (7%)
    pallas_call x1, Pallas kernels, body(): pl.pallas_call(kernel, out_shape=jax.ShapeDtypeStruct(tokens.shape, token...  69 us
    unnamed x19, local copies, waits for them, and re-layouts  3.48 us

profile of v1, /device:TPU:2, one launch (start us, length us, event | category | flops | bytes accessed | tf_op | source)
XLA Modules:
  0.0 74.0 jit_solution(4578181947233630505)
XLA Ops:
  0.0 0.0 copy-start.6
  0.0 0.0 copy-start.3
  0.0 0.7 %reshape.6.gain1 = f32[1,1280]{1,0:T(1,128)S(1)} reshape(f32[1280]{0:T(1024)} %param.12) | data formatting | bytes 10240 | tf_op jit(solution)/shard_map/reshape | solution.py:240
  0.7 0.0 copy-done.6
  0.8 0.0 copy-start.4
  0.8 0.0 copy-start.5
  0.8 1.1 %copy.11.tok = bf16[512,80]{1,0:T(8,128)(2,1)S(1)} copy(bf16[512,80]{0,1:T(8,128)(2,1)} %param.10) | data formatting | bytes 163840 | tf_op args[0]
  1.8 0.0 copy-done.3
  1.9 0.0 copy-start.2
  1.9 0.2 copy.12.wq
  2.1 0.0 copy-done.4
  2.1 0.2 copy.13.wk
  2.3 0.0 copy-done.5
  2.3 0.2 copy.14.wv
  2.5 0.5 copy-done.2
  3.0 0.0 copy-start
  3.0 0.0 copy-start.1
  3.0 1.3 %copy.15.wi = bf16[1280,320]{1,0:T(8,128)(2,1)} copy(bf16[1280,320]{0,1:T(8,128)(2,1)S(1)} %copy-done.2) | data formatting | bytes 1638400 | tf_op args[8]
  4.3 0.0 copy-done
  4.3 0.0 copy-done.1
  4.3 69.0 %shard_map.100 = bf16[512,80]{1,0:T(8,128)(2,1)S(1)} custom-call(bf16[512,80]{1,0:T(8,128)(2,1)S(1)} %copy.11.tok, s32[1,512]{1,0:T(1,128)S(1)} %copy-done.1, f32[1,1280]{1,0:T(1,128)S(1)} %reshape.6.gain1, f32[1,1280]{1,0:T(1,128)S(1)} %reshape.7.gain2, bf16[1280,80]{1,0:T(8,128)(2,1)S(1)} %copy.12.wq, bf16[1280,80]{1,0:T(8,128)(2,1)S(1)} %copy.13.wk, ...), custom_call_target="tpu_custom_call" | custom-call | tf_op jit(solution)/shard_map/pallas_call | solution.py:207
  73.3 0.7 copy.16
  (1 shorter events, 0.0 us)
Async XLA Ops:
  0.0 0.7 %copy-start.6 = (f32[1280]{0:T(1024)S(1)}, f32[1280]{0:T(1024)}, u32[]{:S(2)}) copy-start(f32[1280]{0:T(1024)} %param.17) | copy-start | bytes 15364
  0.0 1.8 %copy-start.3 = (bf16[1280,80]{0,1:T(8,128)(2,1)S(1)}, bf16[1280,80]{0,1:T(8,128)(2,1)}, u32[]{:S(2)}) copy-start(bf16[1280,80]{0,1:T(8,128)(2,1)} %param.13) | copy-start | bytes 614404
  0.8 1.3 %copy-start.4 = (bf16[1280,80]{0,1:T(8,128)(2,1)S(1)}, bf16[1280,80]{0,1:T(8,128)(2,1)}, u32[]{:S(2)}) copy-start(bf16[1280,80]{0,1:T(8,128)(2,1)} %param.14) | copy-start | bytes 614404
  0.8 1.6 %copy-start.5 = (bf16[1280,80]{0,1:T(8,128)(2,1)S(1)}, bf16[1280,80]{0,1:T(8,128)(2,1)}, u32[]{:S(2)}) copy-start(bf16[1280,80]{0,1:T(8,128)(2,1)} %param.15) | copy-start | bytes 614404
  1.9 1.1 %copy-start.2 = (bf16[1280,320]{0,1:T(8,128)(2,1)S(1)}, bf16[1280,320]{0,1:T(8,128)(2,1)}, u32[]{:S(2)}) copy-start(bf16[1280,320]{0,1:T(8,128)(2,1)} %param.18) | copy-start | bytes 2457604
  3.0 1.3 %copy-start = (bf16[80,1280]{1,0:T(8,128)(2,1)S(1)}, bf16[80,1280]{1,0:T(8,128)(2,1)}, u32[]{:S(2)}) copy-start(bf16[80,1280]{1,0:T(8,128)(2,1)} %wo.1) | copy-start | bytes 614404
  3.0 1.3 %copy-start.1 = (s32[1,512]{1,0:T(1,128)S(1)}, s32[1,512]{1,0:T(1,128)}, u32[]{:S(2)}) copy-start(s32[1,512]{1,0:T(1,128)} %mask.1) | copy-start | bytes 6148

commit v2 on v1

--- a/solution.py
+++ b/solution.py
@@ -29,10 +29,30 @@
 
 
 def kernel(
-    tok, mask, gain1, gain2, wq, wk, wv, wo, wi, wb, out,
+    tok_h, mask_h, gain1_h, gain2_h, wq, wk, wv, wo, wi, wb, out,
+    tok, mask, gain1, gain2,
     x1, x2, norm, part, ra, rb, ta, tb, ua, ub, kv, qa, score, prob, place,
-    wqkv_t, wo_t, wi_t, wb_t, g1, g2, send, recv,
+    wqkv_t, wo_v, wi_t, wb_v, wo_t, wb_t, g1, g2, send, recv, load,
 ):
+    loads = [
+        pltpu.make_async_copy(w, v, load.at[i])
+        for i, (w, v) in enumerate(
+            (
+                (mask_h, mask),
+                (tok_h, tok),
+                (gain1_h, gain1),
+                (gain2_h, gain2),
+                (wq, wqkv_t.at[pl.ds(0, HD)]),
+                (wk, wqkv_t.at[pl.ds(HD, HD)]),
+                (wv, wqkv_t.at[pl.ds(2 * HD, HD)]),
+                (wo, wo_v),
+                (wi, wi_t),
+                (wb, wb_v),
+            )
+        )
+    ]
+    for copy in loads:
+        copy.start()
     tp = lax.axis_index("tp")
     tile = lax.axis_index("tile")
     tiles = lax.axis_size("tile")
@@ -70,6 +90,7 @@
 
     low, high = pl.ds(0, CUT), pl.ds(CUT, HD - CUT)
 
+    loads[0].wait()
     flags = mask[...].astype(F32).astype(BF)
     row_i = lax.broadcasted_iota(jnp.int32, (ROWS, ROWS), 0)
     col_i = lax.broadcasted_iota(jnp.int32, (ROWS, ROWS), 1)
@@ -79,8 +100,8 @@
     slot = jnp.where(mask[...] > 0, running - 1.0, -1.0).astype(jnp.int32)
     at = lax.broadcasted_iota(jnp.int32, (LIVE, ROWS), 0) == slot
     place[...] = at.astype(F32).astype(BF)
-    tok_t = tok[...].astype(F32).T.astype(BF)
-    mine = dot(tok_t, place[...], ((1,), (1,))).astype(BF)
+    loads[1].wait()
+    mine = dot(tok[...], place[...], ((1,), (1,))).astype(BF)
     x1[yy, xx] = mine
 
     pl.semaphore_wait(barrier, len(peers))
@@ -98,17 +119,16 @@
 
     first = gather(x1)
 
-    for i, w in enumerate((wq, wk, wv)):
-        wqkv_t[HD * i : HD * (i + 1), :] = w[...].astype(F32).T.astype(BF)
+    for copy in loads[2:]:
+        copy.wait()
     for i in range(D // 128):
         cols = slice(128 * i, 128 * (i + 1))
-        g1[cols, :] = jnp.broadcast_to(gain1[:, cols], (128, 128)).T
-        g2[cols, :] = jnp.broadcast_to(gain2[:, cols], (128, 128)).T
+        g1[cols, :] = jnp.broadcast_to(gain1[cols].reshape(1, 128), (128, 128)).T
+        g2[cols, :] = jnp.broadcast_to(gain2[cols].reshape(1, 128), (128, 128)).T
     rest = gather_rest(x1, first)
-    wo_t[...] = wo[...].astype(F32).T.astype(BF)
+    wo_t[...] = wo_v[...].T
     for i in range(4):
-        wi_t[:, FB * i : FB * (i + 1)] = wi[FB * i : FB * (i + 1), :].astype(F32).T.astype(BF)
-        wb_t[FB * i : FB * (i + 1), :] = wb[:, FB * i : FB * (i + 1)].astype(F32).T.astype(BF)
+        wb_t[FB * i : FB * (i + 1), :] = wb_v[:, FB * i : FB * (i + 1)].T
     finish(rest)
 
     def normalize(buf, gain):
@@ -198,18 +218,22 @@
         for j in range(SIDE):
             part[1, i, j] = block[HD * j : HD * (j + 1)]
     done = (x2[yy, xx].astype(F32) + scatter(1)).astype(BF)
-    out[...] = dot(done, place[...]).T.astype(BF)
+    out[...] = dot(done, place[...]).astype(BF)
 
 
 def body(tokens, mask, ln1_gain, w_query, w_key, w_value, w_out, ln2_gain, w_in, w_back):
-    v = pl.BlockSpec(memory_space=pltpu.VMEM)
+    h = pl.BlockSpec(memory_space=pltpu.HBM)
     n_sem = 64
     return pl.pallas_call(
         kernel,
-        out_shape=jax.ShapeDtypeStruct(tokens.shape, tokens.dtype),
-        in_specs=[v] * 10,
-        out_specs=v,
+        out_shape=jax.ShapeDtypeStruct((HD, ROWS), tokens.dtype),
+        in_specs=[h] * 10,
+        out_specs=pl.BlockSpec(memory_space=pltpu.VMEM),
         scratch_shapes=[
+            pltpu.VMEM((HD, ROWS), BF),
+            pltpu.VMEM((1, ROWS), jnp.int32),
+            pltpu.VMEM((D,), F32),
+            pltpu.VMEM((D,), F32),
             pltpu.VMEM((SIDE, SIDE, HD, LIVE), BF),
             pltpu.VMEM((SIDE, SIDE, HD, LIVE), BF),
             pltpu.VMEM((D, LIVE), BF),
@@ -226,18 +250,21 @@
             pltpu.VMEM((3, LIVE, LIVE), BF),
             pltpu.VMEM((LIVE, ROWS), BF),
             pltpu.VMEM((3 * HD, D), BF),
+            pltpu.VMEM((HD, D), BF),
+            pltpu.VMEM((FB, D), BF),
+            pltpu.VMEM((FB, D), BF),
             pltpu.VMEM((D, HD), BF),
-            pltpu.VMEM((FB, D), BF),
             pltpu.VMEM((D, FB), BF),
             pltpu.VMEM((D, 128), F32),
             pltpu.VMEM((D, 128), F32),
             pltpu.SemaphoreType.DMA((n_sem,)),
             pltpu.SemaphoreType.DMA((n_sem,)),
+            pltpu.SemaphoreType.DMA((10,)),
         ],
         compiler_params=pltpu.CompilerParams(
-            collective_id=0, has_side_effects=True, vmem_limit_bytes=52 * 2**20
+            collective_id=0, has_side_effects=True, vmem_limit_bytes=60 * 2**20
         ),
-    )(tokens, mask, ln1_gain.reshape(1, D), ln2_gain.reshape(1, D), w_query, w_key, w_value, w_out, w_in, w_back)
+    )(tokens.T, mask, ln1_gain, ln2_gain, w_query.T, w_key.T, w_value.T, w_out, w_in.T, w_back).T
 
 
 def solution(mesh):

time: 74.3 us -> 69.9 us (0.941)
  local copies, waits for them, and re-layouts: 4.97 us -> 1.53 us
  Pallas kernels: 69 us -> 68.2 us
    unnamed x19 -> x1, local copies, waits for them, and re-layouts: 3.48 us -> 1.53 us
    pallas_call x1, Pallas kernels: 69 us -> 68.2 us  [body(): pl.pallas_call(kernel, out_shape=jax.ShapeDtypeStruct((HD, ROWS), tokens....]
    reshape x2 -> x0, local copies, waits for them, and re-layouts: 0.75 us -> none  [the longest x1 0.74 us: body(): ln1_gain.reshape(1, D)]
where the time goes in v2:
time: 69.9 us; the launch traced here: 69.7 us
  Pallas kernels  68.2 us (98%)
  local copies, waits for them, and re-layouts  1.53 us (2%)
    pallas_call x1, Pallas kernels, body(): pl.pallas_call(kernel, out_shape=jax.ShapeDtypeStruct((HD, ROWS), tokens....  68.2 us
    unnamed x1, local copies, waits for them, and re-layouts  1.53 us

profile of v2, /device:TPU:2, one launch (start us, length us, event | category | flops | bytes accessed | tf_op | source)
XLA Modules:
  0.0 69.7 jit_solution(7420933497423735998)
XLA Ops:
  0.0 68.2 %shard_map.100 = bf16[80,512]{1,0:T(8,128)(2,1)} custom-call(bf16[80,512]{1,0:T(8,128)(2,1)} %bitcast.11, s32[1,512]{1,0:T(1,128)} %mask_h.1, f32[1280]{0:T(1024)} %gain1_h.1, f32[1280]{0:T(1024)} %gain2_h.1, bf16[80,1280]{1,0:T(8,128)(2,1)} %bitcast.8, bf16[80,1280]{1,0:T(8,128)(2,1)} %bitcast.9, bf16[80,1280]{1,0:T(8,128)(2,1)} %bitcast.10, ...), custom_call_target="tpu_custom_call" | custom-call | tf_op jit(solution)/shard_map/pallas_call | solution.py:227
  68.2 1.5 %copy.12 = bf16[512,80]{0,1:T(8,128)(2,1)} copy(bf16[512,80]{0,1:T(8,128)(2,1)} %bitcast.7) | data formatting | bytes 163840

commit v3 on v2

--- a/solution.py
+++ b/solution.py
@@ -11,6 +11,7 @@
 D = 1280
 FB = 320
 HD = 80
+HALF = 640
 SIDE = 4
 ROWS = 512
 LIVE = 384
@@ -32,8 +33,29 @@
     tok_h, mask_h, gain1_h, gain2_h, wq, wk, wv, wo, wi, wb, out,
     tok, mask, gain1, gain2,
     x1, x2, norm, part, ra, rb, ta, tb, ua, ub, kv, qa, score, prob, place,
-    wqkv_t, wo_v, wi_t, wb_v, wo_t, wb_t, g1, g2, send, recv, load,
+    wqkv_t, w, wi_t, wb_v, w_t, wb_t, og, g1, g2, send, recv, load,
 ):
+    tp = lax.axis_index("tp")
+    tile = lax.axis_index("tile")
+    tiles = lax.axis_size("tile")
+    xx, yy = lax.rem(tp, SIDE), lax.div(tp, SIDE)
+    core = lax.rem(tile, 2)
+    p, q = yy + core * (xx - yy), xx + core * (yy - xx)
+
+    def spot(i):
+        y, x = i // SIDE, i % SIDE
+        return y + core * (x - y), x + core * (y - x)
+
+    def device(p, q):
+        return {"tp": p * (SIDE - 3 * core) + q * (1 + 3 * core)}
+
+    def ppeer(d):
+        return device(lax.rem(p + d, SIDE), q)
+
+    def qpeer(d):
+        return device(p, lax.rem(q + d, SIDE))
+
+    other = {"tile": tile + 1 - 2 * core}
     loads = [
         pltpu.make_async_copy(w, v, load.at[i])
         for i, (w, v) in enumerate(
@@ -45,7 +67,7 @@
                 (wq, wqkv_t.at[pl.ds(0, HD)]),
                 (wk, wqkv_t.at[pl.ds(HD, HD)]),
                 (wv, wqkv_t.at[pl.ds(2 * HD, HD)]),
-                (wo, wo_v),
+                (wo.at[:, pl.ds(pl.multiple_of(core * HALF, 128), HALF)], w.at[core, p, q]),
                 (wi, wi_t),
                 (wb, wb_v),
             )
@@ -53,20 +75,10 @@
     ]
     for copy in loads:
         copy.start()
-    tp = lax.axis_index("tp")
-    tile = lax.axis_index("tile")
-    tiles = lax.axis_size("tile")
-    xx, yy = lax.rem(tp, SIDE), lax.div(tp, SIDE)
-
-    def xpeer(d):
-        return {"tp": yy * SIDE + lax.rem(xx + d, SIDE)}
-
-    def ypeer(d):
-        return {"tp": lax.rem(yy + d, SIDE) * SIDE + xx}
 
     after = {"tile": lax.rem(tile + 1, tiles)}
     before = {"tile": lax.rem(tile + tiles - 1, tiles)}
-    peers = [xpeer(d) for d in (1, 2, 3)] + [ypeer(d) for d in (1, 2, 3)] + [after, before]
+    peers = [ppeer(d) for d in (1, 2, 3)] + [qpeer(d) for d in (1, 2, 3)] + [after, before]
 
     barrier = pltpu.get_barrier_semaphore()
     for peer in peers:
@@ -102,20 +114,24 @@
     place[...] = at.astype(F32).astype(BF)
     loads[1].wait()
     mine = dot(tok[...], place[...], ((1,), (1,))).astype(BF)
-    x1[yy, xx] = mine
+    x1[p, q] = mine
 
     pl.semaphore_wait(barrier, len(peers))
 
-    def gather(buf):
-        first = [push(buf.at[yy, xx, low], buf.at[yy, xx, low], xpeer(d)) for d in (1, 2, 3)]
-        first += [push(buf.at[yy, xx, high], buf.at[yy, xx, high], ypeer(d)) for d in (1, 2, 3)]
-        return first
-
-    def gather_rest(buf, first):
+    def gather(buf, pre=()):
+        def go(part, peer):
+            at = buf.at[(*pre, p, q, part)]
+            return [push(at, at, peer(d)) for d in (1, 2, 3)]
+
+        return go(low, qpeer) + go(high, ppeer)
+
+    def gather_rest(buf, first, pre=()):
+        def go(index, peer):
+            at = buf.at[(*pre, *index)]
+            return [push(at, at, peer(d)) for d in (1, 2, 3)]
+
         finish(first)
-        rest = [push(buf.at[yy, :, low], buf.at[yy, :, low], ypeer(d)) for d in (1, 2, 3)]
-        rest += [push(buf.at[:, xx, high], buf.at[:, xx, high], xpeer(d)) for d in (1, 2, 3)]
-        return rest
+        return go((p, slice(None), low), ppeer) + go((slice(None), q, high), qpeer)
 
     first = gather(x1)
 
@@ -126,14 +142,14 @@
         g1[cols, :] = jnp.broadcast_to(gain1[cols].reshape(1, 128), (128, 128)).T
         g2[cols, :] = jnp.broadcast_to(gain2[cols].reshape(1, 128), (128, 128)).T
     rest = gather_rest(x1, first)
-    wo_t[...] = wo_v[...].T
+    w_first = gather(w, (core,))
     for i in range(4):
         wb_t[FB * i : FB * (i + 1), :] = wb_v[:, FB * i : FB * (i + 1)].T
     finish(rest)
 
-    def normalize(buf, gain):
+    def normalize(buf, gain, where):
         def shard(i):
-            return buf[i // SIDE, i % SIDE].astype(F32)
+            return buf[where(i)].astype(F32)
 
         total = jnp.zeros((HD, LIVE), F32)
         for i in range(16):
@@ -150,7 +166,7 @@
             g = jnp.concatenate([g, g, g], axis=1)
             norm[HD * i : HD * (i + 1), :] = ((shard(i) - mean) * scale * g).astype(BF)
 
-    normalize(x1, g1)
+    normalize(x1, g1, spot)
     qkv = dot(wqkv_t[...], norm[...]).astype(BF)
     valid = lax.broadcasted_iota(jnp.int32, (16, LIVE), 1).astype(F32) < total
     top = lax.broadcasted_iota(jnp.int32, (16, LIVE), 0) == 0
@@ -160,6 +176,7 @@
     kv[1, HD:KB, :] = jnp.where(valid, 0.0, jnp.where(top, LOW, 0.0)).astype(BF)
     kv[1, KB:KV, :] = qkv[2 * HD :]
     halo = [push(kv.at[1], kv.at[0], after), push(kv.at[1], kv.at[2], before)]
+    w_rest = gather_rest(w, w_first, (core,))
     finish(halo)
     edge = jnp.where(top, LOW, 0.0)
     for i, at_edge in ((0, tile == 0), (2, tile == tiles - 1)):
@@ -176,48 +193,64 @@
     weight = jnp.zeros((8, LIVE), F32)
     mixed = jnp.zeros((HD, LIVE), F32)
     for i in range(3):
-        p = jnp.exp2((score[i] - best) * EXPF)
-        weight += jnp.sum(p.reshape(LIVE // 8, 8, LIVE), axis=0)
-        prob[i] = p.astype(BF)
+        e = jnp.exp2((score[i] - best) * EXPF)
+        weight += jnp.sum(e.reshape(LIVE // 8, 8, LIVE), axis=0)
+        prob[i] = e.astype(BF)
         mixed += dot(kv[i, KB:KV, :], prob[i])
     weight = jnp.sum(weight, axis=0, keepdims=True)
     o = (mixed / weight).astype(BF)
 
-    def scatter(n):
-        first = [push(part.at[n, lax.rem(yy + d, SIDE), :, low], ra.at[n, d - 1], ypeer(d)) for d in (1, 2, 3)]
-        first += [push(part.at[n, :, lax.rem(xx + d, SIDE), high], rb.at[n, d - 1], xpeer(d)) for d in (1, 2, 3)]
+    def scatter():
+        first = [push(part.at[lax.rem(p + d, SIDE), :, low], ra.at[d - 1], ppeer(d)) for d in (1, 2, 3)]
+        first += [push(part.at[:, lax.rem(q + d, SIDE), high], rb.at[d - 1], qpeer(d)) for d in (1, 2, 3)]
         finish(first)
-        sum_a = part[n, yy, :, low].astype(F32)
-        sum_b = part[n, :, xx, high].astype(F32)
+        sum_a = part[p, :, low].astype(F32)
+        sum_b = part[:, q, high].astype(F32)
         for d in range(3):
-            sum_a += ra[n, d].astype(F32)
-            sum_b += rb[n, d].astype(F32)
-        ta[n] = sum_a.astype(BF)
-        tb[n] = sum_b.astype(BF)
-        rest = [push(ta.at[n, lax.rem(xx + d, SIDE)], ua.at[n, d - 1], xpeer(d)) for d in (1, 2, 3)]
-        rest += [push(tb.at[n, lax.rem(yy + d, SIDE)], ub.at[n, d - 1], ypeer(d)) for d in (1, 2, 3)]
+            sum_a += ra[d].astype(F32)
+            sum_b += rb[d].astype(F32)
+        ta[...] = sum_a.astype(BF)
+        tb[...] = sum_b.astype(BF)
+        rest = [push(ta.at[lax.rem(q + d, SIDE)], ua.at[d - 1], qpeer(d)) for d in (1, 2, 3)]
+        rest += [push(tb.at[lax.rem(p + d, SIDE)], ub.at[d - 1], ppeer(d)) for d in (1, 2, 3)]
         finish(rest)
-        sum_a = ta[n, xx].astype(F32)
-        sum_b = tb[n, yy].astype(F32)
+        sum_a = ta[q].astype(F32)
+        sum_b = tb[p].astype(F32)
         for d in range(3):
-            sum_a += ua[n, d].astype(F32)
-            sum_b += ub[n, d].astype(F32)
+            sum_a += ua[d].astype(F32)
+            sum_b += ub[d].astype(F32)
         return jnp.concatenate([sum_a, sum_b], axis=0)
 
+    og[p, q] = o
+    o_first = gather(og)
+    finish(w_rest)
+    swap = [push(w.at[core, i], w.at[core, :, i], other) for i in range(SIDE)]
+    o_rest = gather_rest(og, o_first)
+
+    def turn(half):
+        block = w[half].reshape(D, HALF)
+        rows = pl.ds(pl.multiple_of(half * HALF, 128), HALF)
+        for k in range(D // 128):
+            cols = slice(128 * k, 128 * (k + 1))
+            w_t[rows, cols] = block[cols].T
+
+    turn(core)
+    finish(swap)
+    turn(1 - core)
+    finish(o_rest)
+    o_all = og[...].reshape(D, LIVE)
     for i in range(SIDE):
-        block = dot(wo_t[FB * i : FB * (i + 1), :], o).astype(BF)
+        block = dot(w_t[FB * i : FB * (i + 1), :], o_all)
         for j in range(SIDE):
-            part[0, i, j] = block[HD * j : HD * (j + 1)]
-    hidden = (x1[yy, xx].astype(F32) + scatter(0)).astype(BF)
-    x2[yy, xx] = hidden
-    finish(gather_rest(x2, gather(x2)))
-    normalize(x2, g2)
+            token = x1[spot(SIDE * i + j)].astype(F32)
+            x2[i, j] = (token + block[HD * j : HD * (j + 1)]).astype(BF)
+    normalize(x2, g2, lambda i: (i // SIDE, i % SIDE))
     inner = jax.nn.gelu(dot(wi_t[...], norm[...])).astype(BF)
     for i in range(SIDE):
         block = dot(wb_t[FB * i : FB * (i + 1), :], inner).astype(BF)
         for j in range(SIDE):
-            part[1, i, j] = block[HD * j : HD * (j + 1)]
-    done = (x2[yy, xx].astype(F32) + scatter(1)).astype(BF)
+            part[spot(SIDE * i + j)] = block[HD * j : HD * (j + 1)]
+    done = (x2[yy, xx].astype(F32) + scatter()).astype(BF)
     out[...] = dot(done, place[...]).astype(BF)
 
 
@@ -237,24 +270,25 @@
             pltpu.VMEM((SIDE, SIDE, HD, LIVE), BF),
             pltpu.VMEM((SIDE, SIDE, HD, LIVE), BF),
             pltpu.VMEM((D, LIVE), BF),
-            pltpu.VMEM((2, SIDE, SIDE, HD, LIVE), BF),
-            pltpu.VMEM((2, 3, SIDE, CUT, LIVE), BF),
-            pltpu.VMEM((2, 3, SIDE, HD - CUT, LIVE), BF),
-            pltpu.VMEM((2, SIDE, CUT, LIVE), BF),
-            pltpu.VMEM((2, SIDE, HD - CUT, LIVE), BF),
-            pltpu.VMEM((2, 3, CUT, LIVE), BF),
-            pltpu.VMEM((2, 3, HD - CUT, LIVE), BF),
+            pltpu.VMEM((SIDE, SIDE, HD, LIVE), BF),
+            pltpu.VMEM((3, SIDE, CUT, LIVE), BF),
+            pltpu.VMEM((3, SIDE, HD - CUT, LIVE), BF),
+            pltpu.VMEM((SIDE, CUT, LIVE), BF),
+            pltpu.VMEM((SIDE, HD - CUT, LIVE), BF),
+            pltpu.VMEM((3, CUT, LIVE), BF),
+            pltpu.VMEM((3, HD - CUT, LIVE), BF),
             pltpu.VMEM((3, KV, LIVE), BF),
             pltpu.VMEM((KB, LIVE), BF),
             pltpu.VMEM((3, LIVE, LIVE), F32),
             pltpu.VMEM((3, LIVE, LIVE), BF),
             pltpu.VMEM((LIVE, ROWS), BF),
             pltpu.VMEM((3 * HD, D), BF),
-            pltpu.VMEM((HD, D), BF),
+            pltpu.VMEM((2, SIDE, SIDE, HD, HALF), BF),
             pltpu.VMEM((FB, D), BF),
             pltpu.VMEM((FB, D), BF),
-            pltpu.VMEM((D, HD), BF),
+            pltpu.VMEM((D, D), BF),
             pltpu.VMEM((D, FB), BF),
+            pltpu.VMEM((SIDE, SIDE, HD, LIVE), BF),
             pltpu.VMEM((D, 128), F32),
             pltpu.VMEM((D, 128), F32),
             pltpu.SemaphoreType.DMA((n_sem,)),

time: 69.9 us -> 61.8 us (0.88)
  Pallas kernels: 68.2 us -> 60.1 us
    pallas_call x1, Pallas kernels: 68.2 us -> 60.1 us  [body(): pl.pallas_call(kernel, out_shape=jax.ShapeDtypeStruct((HD, ROWS), tokens....]
where the time goes in v3:
time: 61.8 us; the launch traced here: 61.6 us
  Pallas kernels  60.1 us (97%)
  local copies, waits for them, and re-layouts  1.53 us (2%)
    pallas_call x1, Pallas kernels, body(): pl.pallas_call(kernel, out_shape=jax.ShapeDtypeStruct((HD, ROWS), tokens....  60.1 us
    unnamed x1, local copies, waits for them, and re-layouts  1.53 us

profile of v3, /device:TPU:2, one launch (start us, length us, event | category | flops | bytes accessed | tf_op | source)
XLA Modules:
  0.0 61.6 jit_solution(3289211300098444313)
XLA Ops:
  0.0 60.1 %shard_map.100 = bf16[80,512]{1,0:T(8,128)(2,1)} custom-call(bf16[80,512]{1,0:T(8,128)(2,1)} %bitcast.11, s32[1,512]{1,0:T(1,128)} %mask_h.1, f32[1280]{0:T(1024)} %gain1_h.1, f32[1280]{0:T(1024)} %gain2_h.1, bf16[80,1280]{1,0:T(8,128)(2,1)} %bitcast.8, bf16[80,1280]{1,0:T(8,128)(2,1)} %bitcast.9, bf16[80,1280]{1,0:T(8,128)(2,1)} %bitcast.10, ...), custom_call_target="tpu_custom_call" | custom-call | tf_op jit(solution)/shard_map/pallas_call | solution.py:260
  60.1 1.5 %copy.12 = bf16[512,80]{0,1:T(8,128)(2,1)} copy(bf16[512,80]{0,1:T(8,128)(2,1)} %bitcast.7) | data formatting | bytes 163840

commit v4 on v3

--- a/solution.py
+++ b/solution.py
@@ -119,19 +119,23 @@
     pl.semaphore_wait(barrier, len(peers))
 
     def gather(buf, pre=()):
-        def go(part, peer):
-            at = buf.at[(*pre, p, q, part)]
-            return [push(at, at, peer(d)) for d in (1, 2, 3)]
-
-        return go(low, qpeer) + go(high, ppeer)
+        at_low, at_high = buf.at[(*pre, p, q, low)], buf.at[(*pre, p, q, high)]
+        near = [push(at_low, at_low, qpeer(d)) for d in (1, 2, 3)]
+        near += [push(at_high, at_high, ppeer(d)) for d in (1, 2, 3)]
+        own = [push(at_low, at_low, ppeer(d)) for d in (1, 2, 3)]
+        own += [push(at_high, at_high, qpeer(d)) for d in (1, 2, 3)]
+        return near, own
 
     def gather_rest(buf, first, pre=()):
-        def go(index, peer):
-            at = buf.at[(*pre, *index)]
-            return [push(at, at, peer(d)) for d in (1, 2, 3)]
-
-        finish(first)
-        return go((p, slice(None), low), ppeer) + go((slice(None), q, high), qpeer)
+        near, rest = first
+        for d in (1, 2, 3):
+            near[d - 1].wait()
+            at = buf.at[(*pre, p, lax.rem(q + SIDE - d, SIDE), low)]
+            rest = rest + [push(at, at, ppeer(e)) for e in (1, 2, 3)]
+            near[d + 2].wait()
+            at = buf.at[(*pre, lax.rem(p + SIDE - d, SIDE), q, high)]
+            rest = rest + [push(at, at, qpeer(e)) for e in (1, 2, 3)]
+        return rest
 
     first = gather(x1)
 
@@ -256,7 +260,7 @@
 
 def body(tokens, mask, ln1_gain, w_query, w_key, w_value, w_out, ln2_gain, w_in, w_back):
     h = pl.BlockSpec(memory_space=pltpu.HBM)
-    n_sem = 64
+    n_sem = 112
     return pl.pallas_call(
         kernel,
         out_shape=jax.ShapeDtypeStruct((HD, ROWS), tokens.dtype),

time: 61.8 us -> 55.9 us (0.905)
  the two profiles are of different devices: /device:TPU:2 before, /device:TPU:16 now
where the time goes in v4:
time: 55.9 us; the launch traced here: 55.8 us
  Pallas kernels  54.2 us (97%)
  local copies, waits for them, and re-layouts  1.53 us (3%)
    pallas_call x1, Pallas kernels, body(): pl.pallas_call(kernel, out_shape=jax.ShapeDtypeStruct((HD, ROWS), tokens....  54.2 us
    unnamed x1, local copies, waits for them, and re-layouts  1.53 us

profile of v4, /device:TPU:16, one launch (start us, length us, event | category | flops | bytes accessed | tf_op | source)
XLA Modules:
  0.0 55.8 jit_solution(16898782013343283261)
XLA Ops:
  0.0 54.2 %shard_map.100 = bf16[80,512]{1,0:T(8,128)(2,1)} custom-call(bf16[80,512]{1,0:T(8,128)(2,1)} %bitcast.11, s32[1,512]{1,0:T(1,128)} %mask_h.1, f32[1280]{0:T(1024)} %gain1_h.1, f32[1280]{0:T(1024)} %gain2_h.1, bf16[80,1280]{1,0:T(8,128)(2,1)} %bitcast.8, bf16[80,1280]{1,0:T(8,128)(2,1)} %bitcast.9, bf16[80,1280]{1,0:T(8,128)(2,1)} %bitcast.10, ...), custom_call_target="tpu_custom_call" | custom-call | tf_op jit(solution)/shard_map/pallas_call | solution.py:264
  54.2 1.5 %copy.12 = bf16[512,80]{0,1:T(8,128)(2,1)} copy(bf16[512,80]{0,1:T(8,128)(2,1)} %bitcast.7) | data formatting | bytes 163840

commit v5 on v4

--- a/solution.py
+++ b/solution.py
@@ -84,21 +84,21 @@
     for peer in peers:
         pl.semaphore_signal(barrier, inc=1, device_id=peer, device_id_type=MESH)
 
-    count_sems = [0]
+    pushed = []
 
     def push(src, dst, peer):
-        k = count_sems[0]
-        count_sems[0] += 1
+        k = len(pushed)
         copy = pltpu.make_async_remote_copy(
             src_ref=src, dst_ref=dst, send_sem=send.at[k], recv_sem=recv.at[k],
             device_id=peer, device_id_type=MESH,
         )
         copy.start()
+        pushed.append(copy)
         return copy
 
     def finish(copies):
         for copy in copies:
-            copy.wait()
+            copy.wait_recv()
 
     low, high = pl.ds(0, CUT), pl.ds(CUT, HD - CUT)
 
@@ -129,10 +129,10 @@
     def gather_rest(buf, first, pre=()):
         near, rest = first
         for d in (1, 2, 3):
-            near[d - 1].wait()
+            near[d - 1].wait_recv()
             at = buf.at[(*pre, p, lax.rem(q + SIDE - d, SIDE), low)]
             rest = rest + [push(at, at, ppeer(e)) for e in (1, 2, 3)]
-            near[d + 2].wait()
+            near[d + 2].wait_recv()
             at = buf.at[(*pre, lax.rem(p + SIDE - d, SIDE), q, high)]
             rest = rest + [push(at, at, qpeer(e)) for e in (1, 2, 3)]
         return rest
@@ -205,24 +205,35 @@
     o = (mixed / weight).astype(BF)
 
     def scatter():
-        first = [push(part.at[lax.rem(p + d, SIDE), :, low], ra.at[d - 1], ppeer(d)) for d in (1, 2, 3)]
-        first += [push(part.at[:, lax.rem(q + d, SIDE), high], rb.at[d - 1], qpeer(d)) for d in (1, 2, 3)]
-        finish(first)
-        sum_a = part[p, :, low].astype(F32)
-        sum_b = part[:, q, high].astype(F32)
-        for d in range(3):
-            sum_a += ra[d].astype(F32)
-            sum_b += rb[d].astype(F32)
-        ta[...] = sum_a.astype(BF)
-        tb[...] = sum_b.astype(BF)
-        rest = [push(ta.at[lax.rem(q + d, SIDE)], ua.at[d - 1], qpeer(d)) for d in (1, 2, 3)]
-        rest += [push(tb.at[lax.rem(p + d, SIDE)], ub.at[d - 1], ppeer(d)) for d in (1, 2, 3)]
+        early = list(pushed)
+        stage = {}
+        for e in (1, 2, 3, 0):
+            pe, qe = lax.rem(p + e, SIDE), lax.rem(q + e, SIDE)
+            for d in (1, 2, 3):
+                pd, qd = lax.rem(p + d, SIDE), lax.rem(q + d, SIDE)
+                stage[e, d, 0] = push(part.at[pd, qe, low], ra.at[e, d - 1], ppeer(d))
+                stage[e, d, 1] = push(part.at[pe, qd, high], rb.at[e, d - 1], qpeer(d))
+        for copy in early:
+            copy.wait_send()
+        rest = []
+        for e in (1, 2, 3, 0):
+            sum_a = part[p, lax.rem(q + e, SIDE), low].astype(F32)
+            sum_b = part[lax.rem(p + e, SIDE), q, high].astype(F32)
+            for d in (1, 2, 3):
+                finish([stage[e, d, 0], stage[e, d, 1]])
+                sum_a += ra[e, d - 1].astype(F32)
+                sum_b += rb[e, d - 1].astype(F32)
+            if e:
+                ta[e - 1] = sum_a.astype(BF)
+                tb[e - 1] = sum_b.astype(BF)
+                rest.append(push(ta.at[e - 1], ua.at[e - 1], qpeer(e)))
+                rest.append(push(tb.at[e - 1], ub.at[e - 1], ppeer(e)))
         finish(rest)
-        sum_a = ta[q].astype(F32)
-        sum_b = tb[p].astype(F32)
         for d in range(3):
             sum_a += ua[d].astype(F32)
             sum_b += ub[d].astype(F32)
+        for copy in pushed[len(early) :]:
+            copy.wait_send()
         return jnp.concatenate([sum_a, sum_b], axis=0)
 
     og[p, q] = o
@@ -260,7 +271,7 @@
 
 def body(tokens, mask, ln1_gain, w_query, w_key, w_value, w_out, ln2_gain, w_in, w_back):
     h = pl.BlockSpec(memory_space=pltpu.HBM)
-    n_sem = 112
+    n_sem = 128
     return pl.pallas_call(
         kernel,
         out_shape=jax.ShapeDtypeStruct((HD, ROWS), tokens.dtype),
@@ -275,10 +286,10 @@
             pltpu.VMEM((SIDE, SIDE, HD, LIVE), BF),
             pltpu.VMEM((D, LIVE), BF),
             pltpu.VMEM((SIDE, SIDE, HD, LIVE), BF),
-            pltpu.VMEM((3, SIDE, CUT, LIVE), BF),
-            pltpu.VMEM((3, SIDE, HD - CUT, LIVE), BF),
-            pltpu.VMEM((SIDE, CUT, LIVE), BF),
-            pltpu.VMEM((SIDE, HD - CUT, LIVE), BF),
+            pltpu.VMEM((SIDE, 3, CUT, LIVE), BF),
+            pltpu.VMEM((SIDE, 3, HD - CUT, LIVE), BF),
+            pltpu.VMEM((3, CUT, LIVE), BF),
+            pltpu.VMEM((3, HD - CUT, LIVE), BF),
             pltpu.VMEM((3, CUT, LIVE), BF),
             pltpu.VMEM((3, HD - CUT, LIVE), BF),
             pltpu.VMEM((3, KV, LIVE), BF),

time: 55.9 us -> 55.5 us (level)
  the two profiles are of different devices: /device:TPU:16 before, /device:TPU:2 now
where the time goes in v5:
time: 55.5 us; the launch traced here: 55.3 us
  Pallas kernels  53.8 us (97%)
  local copies, waits for them, and re-layouts  1.53 us (3%)
    pallas_call x1, Pallas kernels, body(): pl.pallas_call(kernel, out_shape=jax.ShapeDtypeStruct((HD, ROWS), tokens....  53.8 us
    unnamed x1, local copies, waits for them, and re-layouts  1.53 us

profile of v5, /device:TPU:2, one launch (start us, length us, event | category | flops | bytes accessed | tf_op | source)
XLA Modules:
  0.0 55.3 jit_solution(5777355374972323571)
XLA Ops:
  0.0 53.8 %shard_map.100 = bf16[80,512]{1,0:T(8,128)(2,1)} custom-call(bf16[80,512]{1,0:T(8,128)(2,1)} %bitcast.11, s32[1,512]{1,0:T(1,128)} %mask_h.1, f32[1280]{0:T(1024)} %gain1_h.1, f32[1280]{0:T(1024)} %gain2_h.1, bf16[80,1280]{1,0:T(8,128)(2,1)} %bitcast.8, bf16[80,1280]{1,0:T(8,128)(2,1)} %bitcast.9, bf16[80,1280]{1,0:T(8,128)(2,1)} %bitcast.10, ...), custom_call_target="tpu_custom_call" | custom-call | tf_op jit(solution)/shard_map/pallas_call | solution.py:275
  53.8 1.5 %copy.12 = bf16[512,80]{0,1:T(8,128)(2,1)} copy(bf16[512,80]{0,1:T(8,128)(2,1)} %bitcast.7) | data formatting | bytes 163840

commit v6 on v4

--- a/solution.py
+++ b/solution.py
@@ -84,21 +84,21 @@
     for peer in peers:
         pl.semaphore_signal(barrier, inc=1, device_id=peer, device_id_type=MESH)
 
-    count_sems = [0]
+    pushed = []
 
     def push(src, dst, peer):
-        k = count_sems[0]
-        count_sems[0] += 1
+        k = len(pushed)
         copy = pltpu.make_async_remote_copy(
             src_ref=src, dst_ref=dst, send_sem=send.at[k], recv_sem=recv.at[k],
             device_id=peer, device_id_type=MESH,
         )
         copy.start()
+        pushed.append(copy)
         return copy
 
     def finish(copies):
         for copy in copies:
-            copy.wait()
+            copy.wait_recv()
 
     low, high = pl.ds(0, CUT), pl.ds(CUT, HD - CUT)
 
@@ -120,21 +120,21 @@
 
     def gather(buf, pre=()):
         at_low, at_high = buf.at[(*pre, p, q, low)], buf.at[(*pre, p, q, high)]
-        near = [push(at_low, at_low, qpeer(d)) for d in (1, 2, 3)]
-        near += [push(at_high, at_high, ppeer(d)) for d in (1, 2, 3)]
-        own = [push(at_low, at_low, ppeer(d)) for d in (1, 2, 3)]
-        own += [push(at_high, at_high, qpeer(d)) for d in (1, 2, 3)]
+        near = [push(at_low, at_low, qpeer(d)) for d in (1, 3, 2)]
+        near += [push(at_high, at_high, ppeer(d)) for d in (1, 3, 2)]
+        own = [push(at_low, at_low, ppeer(d)) for d in (1, 3, 2)]
+        own += [push(at_high, at_high, qpeer(d)) for d in (1, 3, 2)]
         return near, own
 
     def gather_rest(buf, first, pre=()):
         near, rest = first
-        for d in (1, 2, 3):
-            near[d - 1].wait()
+        for k, d in enumerate((1, 3, 2)):
+            near[k].wait_recv()
             at = buf.at[(*pre, p, lax.rem(q + SIDE - d, SIDE), low)]
-            rest = rest + [push(at, at, ppeer(e)) for e in (1, 2, 3)]
-            near[d + 2].wait()
+            rest = rest + [push(at, at, ppeer(e)) for e in (1, 3, 2)]
+            near[k + 3].wait_recv()
             at = buf.at[(*pre, lax.rem(p + SIDE - d, SIDE), q, high)]
-            rest = rest + [push(at, at, qpeer(e)) for e in (1, 2, 3)]
+            rest = rest + [push(at, at, qpeer(e)) for e in (1, 3, 2)]
         return rest
 
     first = gather(x1)
@@ -181,14 +181,13 @@
     kv[1, KB:KV, :] = qkv[2 * HD :]
     halo = [push(kv.at[1], kv.at[0], after), push(kv.at[1], kv.at[2], before)]
     w_rest = gather_rest(w, w_first, (core,))
-    finish(halo)
-    edge = jnp.where(top, LOW, 0.0)
-    for i, at_edge in ((0, tile == 0), (2, tile == tiles - 1)):
-        off = jnp.where(at_edge, 1.0, 0.0).astype(F32)
-        kv[i, HD:KB, :] = (kv[i, HD:KB, :].astype(F32) + edge * off).astype(BF)
-
     best = jnp.full((8, LIVE), LOW, F32)
-    for i in range(3):
+    for i in (1, 0, 2):
+        if i != 1:
+            finish([halo[i // 2]])
+            edge = jnp.where(top, LOW, 0.0)
+            off = jnp.where(tile == (0 if i == 0 else tiles - 1), 1.0, 0.0).astype(F32)
+            kv[i, HD:KB, :] = (kv[i, HD:KB, :].astype(F32) + edge * off).astype(BF)
         keys = kv[i, 0:KB, :].astype(F32).T.astype(BF)
         s = dot(keys, qa[...])
         score[i] = s
@@ -205,8 +204,11 @@
     o = (mixed / weight).astype(BF)
 
     def scatter():
+        early = list(pushed)
         first = [push(part.at[lax.rem(p + d, SIDE), :, low], ra.at[d - 1], ppeer(d)) for d in (1, 2, 3)]
         first += [push(part.at[:, lax.rem(q + d, SIDE), high], rb.at[d - 1], qpeer(d)) for d in (1, 2, 3)]
+        for copy in early:
+            copy.wait_send()
         finish(first)
         sum_a = part[p, :, low].astype(F32)
         sum_b = part[:, q, high].astype(F32)
@@ -223,6 +225,8 @@
         for d in range(3):
             sum_a += ua[d].astype(F32)
             sum_b += ub[d].astype(F32)
+        for copy in pushed[len(early) :]:
+            copy.wait_send()
         return jnp.concatenate([sum_a, sum_b], axis=0)
 
     og[p, q] = o
@@ -260,7 +264,7 @@
 
 def body(tokens, mask, ln1_gain, w_query, w_key, w_value, w_out, ln2_gain, w_in, w_back):
     h = pl.BlockSpec(memory_space=pltpu.HBM)
-    n_sem = 112
+    n_sem = 128
     return pl.pallas_call(
         kernel,
         out_shape=jax.ShapeDtypeStruct((HD, ROWS), tokens.dtype),

time: 55.9 us -> 58.2 us (1.041)
  the two profiles are of different devices: /device:TPU:16 before, /device:TPU:2 now
where the time goes in v6:
time: 58.2 us; the launch traced here: 58 us
  Pallas kernels  56.5 us (97%)
  local copies, waits for them, and re-layouts  1.53 us (3%)
    pallas_call x1, Pallas kernels, body(): pl.pallas_call(kernel, out_shape=jax.ShapeDtypeStruct((HD, ROWS), tokens....  56.5 us
    unnamed x1, local copies, waits for them, and re-layouts  1.53 us

profile of v6, /device:TPU:2, one launch (start us, length us, event | category | flops | bytes accessed | tf_op | source)
XLA Modules:
  0.0 58.0 jit_solution(6462334794715252884)
XLA Ops:
  0.0 56.5 %shard_map.100 = bf16[80,512]{1,0:T(8,128)(2,1)} custom-call(bf16[80,512]{1,0:T(8,128)(2,1)} %bitcast.11, s32[1,512]{1,0:T(1,128)} %mask_h.1, f32[1280]{0:T(1024)} %gain1_h.1, f32[1280]{0:T(1024)} %gain2_h.1, bf16[80,1280]{1,0:T(8,128)(2,1)} %bitcast.8, bf16[80,1280]{1,0:T(8,128)(2,1)} %bitcast.9, bf16[80,1280]{1,0:T(8,128)(2,1)} %bitcast.10, ...), custom_call_target="tpu_custom_call" | custom-call | tf_op jit(solution)/shard_map/pallas_call | solution.py:268
  56.5 1.5 %copy.12 = bf16[512,80]{0,1:T(8,128)(2,1)} copy(bf16[512,80]{0,1:T(8,128)(2,1)} %bitcast.7) | data formatting | bytes 163840
